TPU v7x, 256 devices: a whole 4x4x8 slice. The times are simulated.
256 devices in a mesh: dp: 16 (over x_lo, y, core), tensor: 16 (over x_hi, z).
Axes of the slice: x: 4 (x_hi: 2, x_lo: 2; x = x_hi * 2 + x_lo), y: 4, z: 8, core: 2. Of those that a mesh axis runs over, the one named last changes fastest.
Arguments:
- stored: bfloat16 [896, 8192], P('tensor', 'dp'), may hold values from -6 to 6
- row_scale: float32 [896], P('tensor'), may hold values from 0.25 to 4
- out_grad: bfloat16 [896, 8192], P('tensor', 'dp'), may hold values from -1 to 1
- gate_weight: bfloat16 [8192, 28672], P('dp', 'tensor'), may hold values from -0.0625 to 0.0625
- up_weight: bfloat16 [8192, 28672], P('dp', 'tensor'), may hold values from -0.0625 to 0.0625
- down_weight: bfloat16 [28672, 8192], P('tensor', 'dp'), may hold values from -0.03125 to 0.03125
Outputs:
- grad_in: bfloat16 [896, 8192], P('tensor', 'dp')
- grad_gate: bfloat16 [8192, 28672], P('dp', 'tensor')
- grad_up: bfloat16 [8192, 28672], P('dp', 'tensor')
- grad_down: bfloat16 [28672, 8192], P('tensor', 'dp')
All inputs are finite; a program needn't handle non-finite values.
Results may differ from a plain program's by a relative error of at most 0.0071.
Values may be sent and summed in bfloat16 or wider, within the bound.
A program may use at most 128 MiB of HBM per device.

v0:
```python
import jax
import jax.numpy as jnp
from jax import lax
from jax.sharding import PartitionSpec as P


def contract(left, right, left_dim, right_dim):
    return lax.dot_general(
        left, right, (((left_dim,), (right_dim,)), ((), ())), preferred_element_type=jnp.float32
    )


def pointwise(summed, grad_sum, width):
    gate = summed[:, :width]
    upper = summed[:, width:]
    sigmoid_gate = jax.nn.sigmoid(gate)
    activated = gate * sigmoid_gate
    hidden = (activated * upper).astype(jnp.bfloat16)
    d_up = (grad_sum * activated).astype(jnp.bfloat16)
    d_gate = (grad_sum * upper * sigmoid_gate * (1.0 + gate * (1.0 - sigmoid_gate))).astype(
        jnp.bfloat16
    )
    return (hidden, d_gate, d_up)


def body(stored, row_scale, out_grad, gate_weight, up_weight, down_weight):
    width = gate_weight.shape[1]
    local_inputs = (stored.astype(jnp.float32) * row_scale[:, None]).astype(jnp.bfloat16)
    inputs_all, grads_all = (
        lax.all_gather(local_inputs, "tensor", axis=0, tiled=True),
        lax.all_gather(out_grad, "tensor", axis=0, tiled=True),
    )
    rows = inputs_all
    summed_share = lax.psum_scatter(
        jnp.concatenate(
            [
                jnp.dot(rows, gate_weight, preferred_element_type=jnp.float32),
                jnp.dot(rows, up_weight, preferred_element_type=jnp.float32),
            ],
            axis=1,
        ),
        "dp",
        scatter_dimension=0,
        tiled=True,
    )
    rows = grads_all
    grad_share = lax.psum_scatter(
        contract(rows, down_weight, 1, 1), "dp", scatter_dimension=0, tiled=True
    )
    summed, grad_sum = (
        lax.all_gather(summed_share, "dp", axis=0, tiled=True),
        lax.all_gather(grad_share, "dp", axis=0, tiled=True),
    )
    hidden, d_gate, d_up = pointwise(summed, grad_sum, width)
    grad_down = contract(hidden, grads_all, 0, 0).astype(jnp.bfloat16)
    grad_gate = contract(inputs_all, d_gate, 0, 0).astype(jnp.bfloat16)
    grad_up = contract(inputs_all, d_up, 0, 0).astype(jnp.bfloat16)
    grad_in = lax.psum_scatter(
        contract(d_gate, gate_weight, 1, 1) + contract(d_up, up_weight, 1, 1),
        "tensor",
        scatter_dimension=0,
        tiled=True,
    ).astype(jnp.bfloat16)
    return (grad_in, grad_gate, grad_up, grad_down)


def solution(mesh):
    placed = (
        P("tensor", "dp"),
        P("tensor"),
        P("tensor", "dp"),
        P("dp", "tensor"),
        P("dp", "tensor"),
        P("tensor", "dp"),
    )
    return jax.shard_map(
        body,
        mesh=mesh,
        in_specs=placed,
        out_specs=(P("tensor", "dp"), P("dp", "tensor"), P("dp", "tensor"), P("tensor", "dp")),
        check_vma=False,
    )
```

profile of v0, /device:TPU:8, one launch (start us, length us, event | category | flops | bytes accessed | tf_op | source)
XLA Modules:
  0.0 574.8 jit_solution(64296507272945939)
XLA Ops:
  7.2 0.0 reduce-scatter.4.cloned.1.call-start
  7.2 49.5 %all_gather.12 = bf16[896,512]{1,0:T(8,128)(2,1)S(1)} all-gather(bf16[56,512]{1,0:T(8,128)(2,1)} %param.8), channel_id=1, replica_groups=mesh['dp'=16,'tensor'=16] {'tensor'}, dimensions={0}, use_global_device_ids=true | all-gather | bytes 974848 | tf_op jit(solution)/shard_map/all_gather | solution.py:31
  56.7 6.0 %fusion.5 = f32[896,1792]{1,0:T(8,128)} fusion(bf16[896,512]{1,0:T(8,128)(2,1)S(1)} %all_gather.12, bf16[1792,512]{1,0:T(8,128)(2,1)} %param.11), kind=kOutput, calls=%fused_computation.13 | convolution fusion | flops 1644167168 | bytes 9175040 | tf_op jit(solution)/shard_map/dot_general | solution.py:8
  62.8 0.0 reduce-scatter.4.cloned.1.call-update
  62.8 0.0 reduce-scatter.6.cloned.1.call-start
  62.8 0.7 copy-done.7
  63.6 0.1 multiply_convert_fusion.6
  63.7 41.3 %all_gather.14 = bf16[896,512]{1,0:T(8,128)(2,1)S(1)} all-gather(bf16[56,512]{1,0:T(8,128)(2,1)S(1)} %multiply_convert_fusion.6), channel_id=1, replica_groups=mesh['dp'=16,'tensor'=16] {'tensor'}, dimensions={0}, use_global_device_ids=true | all-gather | bytes 974848 | tf_op jit(solution)/shard_map/all_gather | solution.py:30
  105.0 1.8 fusion.6
  106.8 1.8 fusion.7
  108.7 5.2 pad_maximum_fusion
  113.8 0.0 reduce-scatter.6.cloned.1.call-update
  113.9 0.0 all-gather.3.cloned.1.call-start
  113.9 17.3 %reduce-scatter.4.cloned.1.call-done = f32[56,1792]{1,0:T(8,128)} async-done(((f32[896,1792]{1,0:T(8,128)}), f32[56,1792]{1,0:T(8,128)}) %reduce-scatter.4.cloned.1.call-update) | async-done | bytes 401424 | tf_op jit(solution)/shard_map/reduce_scatter | solution.py:47
  131.3 0.0 all-gather.3.cloned.1.call-update
  131.3 0.0 all-gather.5.cloned.1.call-start
  131.3 83.8 %reduce-scatter.6.cloned.1.call-done = f32[56,3584]{1,0:T(8,128)} async-done(((f32[896,3584]{1,0:T(8,128)}), f32[56,3584]{1,0:T(8,128)}) %reduce-scatter.6.cloned.1.call-update) | async-done | bytes 802832 | tf_op jit(solution)/shard_map/reduce_scatter | solution.py:34
  215.1 0.0 all-gather.5.cloned.1.call-update
  215.1 0.2 reduce-scatter.8.cloned.1.call-start
  215.4 50.7 %all-gather.3.cloned.1.call-done = f32[896,1792]{1,0:T(8,128)} async-done(((f32[56,1792]{1,0:T(8,128)}), f32[896,1792]{1,0:T(8,128)}) %all-gather.3.cloned.1.call-update) | async-done | bytes 6422544 | tf_op jit(solution)/shard_map/all_gather | solution.py:52
  266.1 78.5 %all-gather.5.cloned.1.call-done = f32[896,3584]{1,0:T(8,128)} async-done(((f32[56,3584]{1,0:T(8,128)}), f32[896,3584]{1,0:T(8,128)}) %all-gather.5.cloned.1.call-update) | async-done | bytes 12845072 | tf_op jit(solution)/shard_map/all_gather | solution.py:51
  344.6 8.1 %multiply_convert_fusion.1 = (bf16[896,1792]{1,0:T(8,128)(2,1)S(1)}, bf16[896,1792]{1,0:T(8,128)(2,1)S(1)}) fusion(f32[896,1792]{1,0:T(8,128)} %all-gather.3.cloned.1.call-done, f32[896,3584]{1,0:T(8,128)} %all-gather.5.cloned.1.call-done), kind=kLoop, calls=%fused_computation.2 | loop fusion | flops 20873216 | bytes 25690112 | tf_op jit(solution)/shard_map/convert_element_type | solution.py:19
  352.7 1.8 fusion.8
  354.6 0.9 copy-done.4
  355.5 0.1 copy-done.10
  355.6 3.1 convolution_add_fusion
  358.7 0.0 reduce-scatter.8.cloned.1.call-update
  358.8 5.4 convolution_convert_fusion
  364.1 3.4 convolution_convert_fusion.1
  367.5 8.4 %fusion.2 = bf16[1792,512]{1,0:T(8,128)(2,1)} fusion(bf16[896,512]{1,0:T(8,128)(2,1)S(1)} %all_gather.12, f32[896,3584]{1,0:T(8,128)} %all-gather.5.cloned.1.call-done), kind=kOutput, calls=%fused_computation.7 | convolution fusion | flops 1654718464 | bytes 15597568 | tf_op jit(solution)/shard_map/dot_general | solution.py:8
  375.9 190.8 %reduce-scatter.8.cloned.1.call-done = f32[56,512]{1,0:T(8,128)} async-done(((f32[896,512]{1,0:T(8,128)}), f32[56,512]{1,0:T(8,128)}) %reduce-scatter.8.cloned.1.call-update) | async-done | bytes 114704 | tf_op jit(solution)/shard_map/reduce_scatter | solution.py:58
  566.7 1.5 convert_element_type.31
  (19 shorter events, 0.0 us)
Async XLA Ops:
  7.2 97.8 %copy-start = (bf16[512,1792]{1,0:T(8,128)(2,1)S(1)}, bf16[512,1792]{1,0:T(8,128)(2,1)}, u32[]{:S(2)}) copy-start(bf16[512,1792]{1,0:T(8,128)(2,1)} %param.9) | copy-start | bytes 5505028
  7.2 124.1 %reduce-scatter.4.cloned.1.call-start = ((), (), s32[]{:S(2)}) async-start(), calls=%async_computation.3 | async-start | bytes 6823936 | tf_op jit(solution)/shard_map/reduce_scatter | solution.py:47
  62.8 0.8 copy-start.7
  62.8 0.8 copy-start.8
  62.8 152.3 %reduce-scatter.6.cloned.1.call-start = ((), (), s32[]{:S(2)}) async-start(), calls=%async_computation.5 | async-start | bytes 13647872 | tf_op jit(solution)/shard_map/reduce_scatter | solution.py:34
  105.0 1.8 copy-start.5
  105.0 1.8 copy-start.9
  113.9 152.2 %all-gather.3.cloned.1.call-start = ((), (), s32[]{:S(2)}) async-start(), calls=%async_computation.4 | async-start | bytes 6823936 | tf_op jit(solution)/shard_map/all_gather | solution.py:52
  131.3 213.3 %all-gather.5.cloned.1.call-start = ((), (), s32[]{:S(2)}) async-start(), calls=%async_computation.6 | async-start | bytes 13647872 | tf_op jit(solution)/shard_map/all_gather | solution.py:51
  215.1 351.6 %reduce-scatter.8.cloned.1.call-start = ((), (), s32[]{:S(2)}) async-start(), calls=%async_computation.7 | async-start | bytes 1949696 | tf_op jit(solution)/shard_map/reduce_scatter | solution.py:58
  352.7 1.9 copy-start.2
  352.7 2.8 copy-start.4
  352.7 2.9 copy-start.10
  355.6 3.1 copy-start.6
  358.7 5.4 copy-start.3
  367.5 200.7 %copy-start.1 = (bf16[512,1792]{1,0:T(8,128)(2,1)S(1)}, bf16[512,1792]{1,0:T(8,128)(2,1)}, u32[]{:S(2)}) copy-start(bf16[512,1792]{1,0:T(8,128)(2,1)} %param.9) | copy-start | bytes 5505028
Sparse Core Ops, SparseCore 0:
  62.9 68.3 reduce-scatter.3
  133.8 81.2 reduce-scatter.5
  217.1 48.8 all-gather.2
  267.9 76.6 all-gather.4
  358.9 207.8 reduce-scatter.7
where the time goes:
time: 575 us
  waiting for transfers between devices  421 us (73%)
  blocking collectives  90.8 us (16%)
  matrix products  31.7 us (6%)
  other arithmetic  14.9 us (3%)
  between operations  13.9 us (2%)
    reduce_scatter x1, waiting for transfers between devices, body(): lax.psum_scatter(contract(d_gate, gate_weight, 1, 1) + contract(d_up, up_...  191 us
    reduce_scatter x1, waiting for transfers between devices, body(): lax.psum_scatter(jnp.concatenate([jnp.dot(rows, gate_weight, preferred_el...  83.8 us
    all_gather x1, waiting for transfers between devices, body(): lax.all_gather(summed_share, 'dp', axis=0, tiled=True)  78.5 us
    all_gather x1, waiting for transfers between devices, body(): lax.all_gather(grad_share, 'dp', axis=0, tiled=True)  50.7 us
    all_gather x1, blocking collectives, body(): lax.all_gather(out_grad, 'tensor', axis=0, tiled=True)  49.5 us
    all_gather x1, blocking collectives, body(): lax.all_gather(local_inputs, 'tensor', axis=0, tiled=True)  41.3 us
    dot_general x6, matrix products, contract(): lax.dot_general(left, right, (((left_dim,), (right_dim,)), ((), ())), pre...  28.1 us
    reduce_scatter x1, waiting for transfers between devices, body(): lax.psum_scatter(contract(rows, down_weight, 1, 1), 'dp', scatter_dimensi...  17.3 us
  transfers between devices with their start and end apart: 5, of which 5 were waited for; matrix products, arithmetic and copies ran while one was open for 5% of the time, Pallas kernels for 0%

commit v1 on v0

v1 whole, which is shorter than its diff:
```python
import jax
import jax.numpy as jnp
from jax import lax
from jax.experimental import pallas as pl
from jax.experimental.pallas import tpu as pltpu
from jax.sharding import PartitionSpec as P

MESH = pl.DeviceIdType.MESH
BF, F32 = jnp.bfloat16, jnp.float32
COPIES = 420
FIRST = "ABABABA"


def dot(a, b):
    return lax.dot_general(a, b, (((1,), (0,)), ((), ())), preferred_element_type=F32)


def dot_t(a, b):
    return lax.dot_general(a, b, (((1,), (1,)), ((), ())), preferred_element_type=F32)


def tdot(a, b):
    return lax.dot_general(a, b, (((0,), (0,)), ((), ())), preferred_element_type=F32)


def kernel(
    own, wg, wu, wd,
    grad_in, grad_gate, grad_up, grad_down,
    blocks, x, px, xt, own_gu, own_d, peer_gu, peer_d, full_g, full_u,
    part, stage, landed, full, tile_g, tile_u, tile_d, total, tail_s, tail_r, tail_h,
    send_sem, recv_sem, load_sem,
):
    d, t = lax.axis_index("dp"), lax.axis_index("tensor")
    c, y, xl = d % 2, (d // 2) % 4, d // 8
    z, h = t % 8, t // 8
    units = part.shape[0]
    y_up, y_down, y_far = (y + 1) % 4, (y + 3) % 4, (y + 2) % 4
    peer = ((xl * 4 + y) * 2 + 1 - c, t)
    across = (((1 - xl) * 4 + y) * 2 + c, t)
    ups = ((xl * 4 + y_up) * 2 + c, t)
    downs = ((xl * 4 + y_down) * 2 + c, t)
    z_up = (d, h * 8 + (z + 1) % 8)
    z_down = (d, h * 8 + (z + 7) % 8)
    twin = (d, (1 - h) * 8 + z)
    everyone = (peer, across, ups, downs, z_up, z_down, twin)

    barrier = pltpu.get_barrier_semaphore()
    for device in everyone:
        pl.semaphore_signal(barrier, inc=1, device_id=device, device_id_type=MESH)

    index, sent, loads = {}, [], []

    def send(key, src, dst, device):
        i = index[key] = len(index)
        copy = pltpu.make_async_remote_copy(
            src_ref=src, dst_ref=dst, send_sem=send_sem.at[i], recv_sem=recv_sem.at[i],
            device_id=device, device_id_type=MESH,
        )
        copy.start()
        sent.append(copy)

    def arrive(key, dst):
        i = index[key]
        pltpu.make_async_remote_copy(
            src_ref=dst, dst_ref=dst, send_sem=send_sem.at[i], recv_sem=recv_sem.at[i],
            device_id=peer, device_id_type=MESH,
        ).wait_recv()

    def load(src, dst):
        copy = pltpu.make_async_copy(src, dst, load_sem.at[len(loads)])
        copy.start()
        loads.append(copy)
        return copy

    def cols(u, core):
        return pl.ds(pl.multiple_of(u * 256 + core * 128, 128), 128)

    own_loads = []
    for u in range(units):
        own_loads.append((
            load(wg.at[:, cols(u, c)], own_gu.at[u, :, pl.ds(0, 128)]),
            load(wu.at[:, cols(u, c)], own_gu.at[u, :, pl.ds(128, 128)]),
            load(wd.at[cols(u, c), :], own_d.at[u]),
        ))
    whole_loads = (load(wg, full_g), load(wu, full_u))
    for a in range(2):
        blocks[a, t] = own[a]

    pl.semaphore_wait(barrier, len(everyone))

    def rank(hh, zz):
        return ((h + hh) % 2) * 8 + zz

    def ring_send(a, hh, step, src_z):
        src = blocks.at[a, rank(hh, src_z)]
        return src

    far = {("+", 0): 4, ("-", 0): 3, ("+", 1): 3, ("-", 1): 4}
    for a in range(2):
        send(("+", a, 0, 1), own.at[a], blocks.at[a, t], z_up)
        send(("-", a, 0, 1), own.at[a], blocks.at[a, t], z_down)
        send(("h", a), own.at[a], blocks.at[a, t], twin)

    def peer_weights(u):
        send(("wg", u), wg.at[:, cols(u, 1 - c)], peer_gu.at[u, :, pl.ds(0, 128)], peer)
        send(("wu", u), wu.at[:, cols(u, 1 - c)], peer_gu.at[u, :, pl.ds(128, 128)], peer)
        send(("wd", u), wd.at[cols(u, 1 - c), :], peer_d.at[u], peer)

    for u in range(units):
        peer_weights(u)

    def ring_step(a, s):
        if s == 0:
            block = blocks.at[a, rank(1, z)]
            arrive(("h", a), block)
            send(("+", a, 1, 1), block, block, z_up)
            send(("-", a, 1, 1), block, block, z_down)
            return
        for hh in range(2):
            for way, device in (("+", z_up), ("-", z_down)):
                if s > far[way, hh]:
                    continue
                zz = (z + 8 - s) % 8 if way == "+" else (z + s) % 8
                block = blocks.at[a, rank(hh, zz)]
                arrive((way, a, hh, s), block)
                if s < far[way, hh]:
                    send((way, a, hh, s + 1), block, block, device)

    def repack(a):
        for k in range(8):
            rows = pl.ds(k * 112, 112)
            pair = [blocks[a, 2 * k + i].astype(F32)[:56] for i in range(2)]
            x[a, rows] = jnp.concatenate(pair, axis=0).astype(BF)
            send(("px", a, k), x.at[a, rows], px.at[a, rows], peer)

    for s in range(6):
        if s < 5:
            ring_step(0, s)
        if s == 5:
            repack(0)
        if s > 0:
            ring_step(1, s - 1)
    repack(1)
    for k in range(7):
        xt[:, k * 128 : (k + 1) * 128] = x[0, k * 128 : (k + 1) * 128].T
    for a in range(2):
        for k in range(8):
            arrive(("px", a, k), px.at[a, pl.ds(k * 112, 112)])

    def forward(u):
        for copy in own_loads[u]:
            copy.wait()
        arrive(("wg", u), peer_gu.at[u, :, pl.ds(0, 128)])
        arrive(("wu", u), peer_gu.at[u, :, pl.ds(128, 128)])
        arrive(("wd", u), peer_d.at[u])

        def rows_of(i, carry):
            rows = pl.ds(pl.multiple_of(i * 224, 224), 224)
            gu = dot(x[0, rows], own_gu[u]) + dot(px[0, rows], peer_gu[u])
            hg = dot_t(x[1, rows], own_d[u]) + dot_t(px[1, rows], peer_d[u])
            for j in range(2):
                part[u, 2 * i + j, :, 0:256] = gu[j * 112 : (j + 1) * 112]
                part[u, 2 * i + j, :, 256:384] = hg[j * 112 : (j + 1) * 112]
            return carry

        lax.fori_loop(0, 4, rows_of, 0)

    def pointwise(u, summed):
        gate, upper, grad = summed[:, :128], summed[:, 128:256], summed[:, 256:]
        sig = lax.logistic(gate)
        activated = gate * sig
        q = y * 2 + xl
        full[u, c, q, :, 0:128] = (activated * upper).astype(BF)
        full[u, c, q, :, 128:256] = (grad * upper * sig * (1.0 + gate * (1.0 - sig))).astype(BF)
        full[u, c, q, :, 256:384] = (grad * activated).astype(BF)

    def to_peer(u, q, name):
        send(("c", u, name), full.at[u, c, q], full.at[u, c, q], peer)

    def stage_a(u, s):
        st, rb = stage.at[u], landed.at[u]
        if s == 0:
            forward(u)
            for k, q, device in (
                (0, y_far * 2, ups), (1, y_far * 2 + 1, downs),
                (2, y_up * 2 + 1, ups), (3, y_down * 2, downs),
            ):
                stage[u, k] = part[u, q].astype(BF)
                send(("r", u, k), st.at[k], rb.at[k], device)
        if s == 1:
            for k, q, device in ((0, y_up * 2, ups), (1, y_down * 2 + 1, downs)):
                arrive(("r", u, k), rb.at[k])
                stage[u, 4 + k] = (part[u, q] + landed[u, k].astype(F32)).astype(BF)
                send(("r", u, 4 + k), st.at[4 + k], rb.at[4 + k], device)
        if s == 2:
            for k in (2, 3, 4, 5):
                arrive(("r", u, k), rb.at[k])
            low = part[u, 2 * y] + (landed[u, 4].astype(F32) + landed[u, 3].astype(F32))
            high = part[u, 2 * y + 1] + (landed[u, 2].astype(F32) + landed[u, 5].astype(F32))
            stage[u, 6] = jnp.where(xl == 0, high, low).astype(BF)
            send(("r", u, 6), st.at[6], rb.at[6], across)
            part[u, 2 * y + xl] = jnp.where(xl == 0, low, high)
        if s == 3:
            arrive(("r", u, 6), rb.at[6])
            pointwise(u, part[u, 2 * y + xl] + landed[u, 6].astype(F32))
            mine = full.at[u, c, 2 * y + xl]
            send(("x", u), mine, mine, across)
            send(("u", u, 0), mine, mine, ups)
            send(("d", u, 0), mine, mine, downs)
            to_peer(u, 2 * y + xl, 0)
        if s == 4:
            other = full.at[u, c, 2 * y + 1 - xl]
            arrive(("x", u), other)
            send(("u", u, 1), other, other, ups)
            send(("d", u, 1), other, other, downs)
            to_peer(u, 2 * y + 1 - xl, 1)
        if s == 5:
            for i in range(2):
                e = xl if i == 0 else 1 - xl
                arrive(("u", u, i), full.at[u, c, 2 * y_down + e])
                arrive(("d", u, i), full.at[u, c, 2 * y_up + e])
            low, high = full.at[u, c, 2 * y_down], full.at[u, c, 2 * y_up + 1]
            send(("u", u, 2), low, low, ups)
            send(("d", u, 2), high, high, downs)
            for i in range(2):
                to_peer(u, 2 * y_down + i, 2 + i)
                to_peer(u, 2 * y_up + i, 4 + i)
        if s == 6:
            arrive(("u", u, 2), full.at[u, c, 2 * y_far])
            arrive(("d", u, 2), full.at[u, c, 2 * y_far + 1])
            for i in range(2):
                to_peer(u, 2 * y_far + i, 6 + i)
        if s == 7:
            for i, q in enumerate((
                2 * y + xl, 2 * y + 1 - xl, 2 * y_down, 2 * y_down + 1,
                2 * y_up, 2 * y_up + 1, 2 * y_far, 2 * y_far + 1,
            )):
                arrive(("c", u, i), full.at[u, 1 - c, q])
            backward(u)

    lo, hi = pl.ds(0, 64), pl.ds(64, 48)

    def stage_b(u, s):
        st, rb = stage.at[u], landed.at[u]
        if s == 0:
            forward(u)
            for k, yy in enumerate((y_far, y_up, y_down, y)):
                stage[u, k] = part[u, yy * 2 + 1 - xl].astype(BF)
                send(("r", u, k), st.at[k], rb.at[k], across)
        if s == 1:
            for k, yy in enumerate((y_far, y_up, y_down, y)):
                arrive(("r", u, k), rb.at[k])
                summed = part[u, yy * 2 + xl] + landed[u, k].astype(F32)
                if k > 0:
                    part[u, yy * 2 + xl] = summed
                if k < 3:
                    stage[u, 4 + k] = summed.astype(BF)
                if k == 0:
                    send(("f", u, 0), st.at[4, lo], rb.at[4, lo], ups)
                    send(("f", u, 1), st.at[4, hi], rb.at[4, hi], downs)
                if k == 1:
                    send(("n", u, 0), st.at[5, hi], rb.at[5, hi], ups)
                if k == 2:
                    send(("n", u, 1), st.at[6, lo], rb.at[6, lo], downs)
        if s == 2:
            arrive(("f", u, 0), rb.at[4, lo])
            stage[u, 5, 0:64] = (
                part[u, y_up * 2 + xl, 0:64] + landed[u, 4, 0:64].astype(F32)
            ).astype(BF)
            send(("n", u, 2), st.at[5, lo], rb.at[5, lo], ups)
            arrive(("f", u, 1), rb.at[4, hi])
            stage[u, 6, 64:112] = (
                part[u, y_down * 2 + xl, 64:112] + landed[u, 4, 64:112].astype(F32)
            ).astype(BF)
            send(("n", u, 3), st.at[6, hi], rb.at[6, hi], downs)
        if s == 3:
            arrive(("n", u, 0), rb.at[5, hi])
            arrive(("n", u, 1), rb.at[6, lo])
            arrive(("n", u, 2), rb.at[5, lo])
            arrive(("n", u, 3), rb.at[6, hi])
            pointwise(u, part[u, 2 * y + xl] + (landed[u, 5].astype(F32) + landed[u, 6].astype(F32)))
            mine = full.at[u, c, 2 * y + xl]
            send(("u", u, 0), mine, mine, ups)
            send(("d", u, 0), mine, mine, downs)
            send(("x", u, 0), mine, mine, across)
            to_peer(u, 2 * y + xl, 0)
        if s == 4:
            low, high = full.at[u, c, 2 * y_down + xl], full.at[u, c, 2 * y_up + xl]
            arrive(("u", u, 0), low)
            send(("u", u, 1), low.at[lo], low.at[lo], ups)
            arrive(("d", u, 0), high)
            send(("d", u, 1), high.at[hi], high.at[hi], downs)
            send(("x", u, 1), low, low, across)
            send(("x", u, 2), high, high, across)
            to_peer(u, 2 * y_down + xl, 1)
            to_peer(u, 2 * y_up + xl, 2)
        if s == 5:
            opposite = full.at[u, c, 2 * y_far + xl]
            arrive(("u", u, 1), opposite.at[lo])
            arrive(("d", u, 1), opposite.at[hi])
            send(("x", u, 3), opposite, opposite, across)
            to_peer(u, 2 * y_far + xl, 3)
        order = (y, y_down, y_up, y_far)
        if s == 6:
            for i, yy in enumerate(order):
                arrive(("x", u, i), full.at[u, c, 2 * yy + 1 - xl])
                to_peer(u, 2 * yy + 1 - xl, 4 + i)
        if s == 7:
            for i, yy in enumerate(order):
                arrive(("c", u, i), full.at[u, 1 - c, 2 * yy + xl])
                arrive(("c", u, 4 + i), full.at[u, 1 - c, 2 * yy + 1 - xl])
            backward(u)

    writes = []

    def backward(u):
        wide = slice(u * 256, (u + 1) * 256)

        def lanes(k, groups=pl.ds(0, 8)):
            both = [full[u, core, groups, :, k * 128 : (k + 1) * 128] for core in range(2)]
            return jnp.concatenate([b.reshape(-1, 128) for b in both], axis=1)

        if u == 0:
            for copy in whole_loads:
                copy.wait()

        def rows_of(i, carry):
            rows = pl.ds(pl.multiple_of(i * 224, 224), 224)
            groups = pl.ds(2 * i, 2)
            term = dot_t(lanes(1, groups), full_g[:, wide]) + dot_t(lanes(2, groups), full_u[:, wide])
            total[rows] = term if u == 0 else total[rows] + term
            return carry

        lax.fori_loop(0, 4, rows_of, 0)

        def depth_of(i, carry):
            rows = pl.ds(pl.multiple_of(i * 256, 256), 256)
            tile_g[u, rows] = dot(xt[rows], lanes(1)).astype(BF)
            tile_u[u, rows] = dot(xt[rows], lanes(2)).astype(BF)
            return carry

        lax.fori_loop(0, 2, depth_of, 0)
        tile_d[u] = tdot(lanes(0), x[1]).astype(BF)
        writes.append(load(tile_g.at[u], grad_gate.at[:, pl.ds(u * 256, 256)]))
        writes.append(load(tile_u.at[u], grad_up.at[:, pl.ds(u * 256, 256)]))
        writes.append(load(tile_d.at[u], grad_down.at[pl.ds(u * 256, 256), :]))

    for tick in range(units + 7):
        for u in range(units):
            s = tick - u
            if 1 <= s <= 6:
                (stage_a if FIRST[u] == "A" else stage_b)(u, s)
        for s in (0, 7):
            u = tick - s
            if 0 <= u < units:
                (stage_a if FIRST[u] == "A" else stage_b)(u, s)

    def block_of(hh, zz):
        return total[pl.ds(pl.multiple_of((hh * 8 + zz) * 56, 8), 56)]

    def padded(value):
        return jnp.concatenate([value, jnp.zeros((8, value.shape[1]), F32)], axis=0).astype(BF)

    def tail_send(way, k, hh, add):
        device, zz = (z_up, (z + k) % 8) if way == 0 else (z_down, (z + 8 - k) % 8)
        value = block_of(hh, zz)
        if add:
            arrive(("t", way, k + 1, hh), tail_r.at[way, k, hh])
            value = value + tail_r[way, k, hh].astype(F32)[:56]
        tail_s[way, k - 1, hh] = padded(value)
        send(("t", way, k, hh), tail_s.at[way, k - 1, hh], tail_r.at[way, k - 1, hh], device)

    tail_send(0, 4, 0, False)
    tail_send(1, 4, 1, False)
    tail_send(0, 3, 1, False)
    tail_send(1, 3, 0, False)
    tail_send(0, 3, 0, True)
    tail_send(1, 3, 1, True)
    for k in (2, 1):
        for hh in ((1, 0), (0, 1)):
            for way in range(2):
                tail_send(way, k, hh[way], True)
    for hh in range(2):
        for way in range(2):
            arrive(("t", way, 1, hh), tail_r.at[way, 0, hh])

    def summed(hh):
        both = tail_r[0, 0, hh].astype(F32) + tail_r[1, 0, hh].astype(F32)
        return block_of(hh, z) + both[:56]

    tail_h[0] = padded(summed(1 - h))
    send(("twin",), tail_h.at[0], tail_h.at[1], twin)
    mine = summed(h)
    arrive(("twin",), tail_h.at[1])
    grad_in[...] = (mine + tail_h[1].astype(F32)[:56]).astype(BF)

    for copy in sent:
        copy.wait_send()
    for copy in writes:
        copy.wait()


def body(stored, row_scale, out_grad, gate_weight, up_weight, down_weight):
    tokens, depth = stored.shape
    width = gate_weight.shape[1]
    units = width // 256
    inputs = (stored.astype(F32) * row_scale[:, None]).astype(BF)
    pad = ((0, 64 - tokens), (0, 0))
    own = jnp.stack([jnp.pad(inputs, pad), jnp.pad(out_grad, pad)])
    everything = tokens * 16
    anywhere, vmem = pl.BlockSpec(memory_space=pl.ANY), pl.BlockSpec(memory_space=pltpu.VMEM)
    dma = pltpu.SemaphoreType.DMA
    return pl.pallas_call(
        kernel,
        out_shape=(
            jax.ShapeDtypeStruct((tokens, depth), BF),
            jax.ShapeDtypeStruct((depth, width), BF),
            jax.ShapeDtypeStruct((depth, width), BF),
            jax.ShapeDtypeStruct((width, depth), BF),
        ),
        in_specs=[vmem, anywhere, anywhere, anywhere],
        out_specs=(vmem, anywhere, anywhere, anywhere),
        scratch_shapes=[
            pltpu.VMEM((2, 16, 64, depth), BF),
            pltpu.VMEM((2, everything, depth), BF),
            pltpu.VMEM((2, everything, depth), BF),
            pltpu.VMEM((depth, everything), BF),
            pltpu.VMEM((units, depth, 256), BF),
            pltpu.VMEM((units, 128, depth), BF),
            pltpu.VMEM((units, depth, 256), BF),
            pltpu.VMEM((units, 128, depth), BF),
            pltpu.VMEM((depth, width), BF),
            pltpu.VMEM((depth, width), BF),
            pltpu.VMEM((units, 8, 112, 384), F32),
            pltpu.VMEM((units, 7, 112, 384), BF),
            pltpu.VMEM((units, 7, 112, 384), BF),
            pltpu.VMEM((units, 2, 8, 112, 384), BF),
            pltpu.VMEM((units, depth, 256), BF),
            pltpu.VMEM((units, depth, 256), BF),
            pltpu.VMEM((units, 256, depth), BF),
            pltpu.VMEM((everything, depth), F32),
            pltpu.VMEM((2, 4, 2, 64, depth), BF),
            pltpu.VMEM((2, 4, 2, 64, depth), BF),
            pltpu.VMEM((2, 64, depth), BF),
            dma((COPIES,)),
            dma((COPIES,)),
            dma((60,)),
        ],
        compiler_params=pltpu.CompilerParams(
            collective_id=0, has_side_effects=True, vmem_limit_bytes=62 * 2**20
        ),
        cost_estimate=pl.CostEstimate(
            flops=16 * everything * depth * width, bytes_accessed=12 * depth * width, transcendentals=0
        ),
    )(own, gate_weight, up_weight, down_weight)


def solution(mesh):
    placed = (
        P("tensor", "dp"),
        P("tensor"),
        P("tensor", "dp"),
        P("dp", "tensor"),
        P("dp", "tensor"),
        P("tensor", "dp"),
    )
    return jax.shard_map(
        body,
        mesh=mesh,
        in_specs=placed,
        out_specs=(P("tensor", "dp"), P("dp", "tensor"), P("dp", "tensor"), P("tensor", "dp")),
        check_vma=False,
    )
```

time: 575 us -> 162 us (0.28)
  waiting for transfers between devices: 421 us -> 0 us
  Pallas kernels: 0 us -> 150 us
  blocking collectives: 90.8 us -> 0 us
  matrix products: 31.7 us -> 0 us
  other arithmetic: 14.9 us -> 1.57 us
  between operations: 13.9 us -> 0.65 us
  local copies, waits for them, and re-layouts: 1.81 us -> 8.65 us
    reduce_scatter x3 -> x0, waiting for transfers between devices: 292 us -> none  [the longest x1 191 us: body(): lax.psum_scatter(contract(d_gate, gate_weight, 1, 1) + contract(d_up, up_...]
    pallas_call x0 -> x1, Pallas kernels: none -> 150 us  [body(): pl.pallas_call(kernel, out_shape=(jax.ShapeDtypeStruct((tokens, depth), B...]
    all_gather x2 -> x0, waiting for transfers between devices: 129 us -> none  [the longest x1 78.5 us: body(): lax.all_gather(summed_share, 'dp', axis=0, tiled=True)]
    all_gather x2 -> x0, blocking collectives: 90.8 us -> none  [the longest x1 49.5 us: body(): lax.all_gather(out_grad, 'tensor', axis=0, tiled=True)]
    dot_general x8 -> x0, matrix products: 31.7 us -> none  [the longest x6 28.1 us: contract(): lax.dot_general(left, right, (((left_dim,), (right_dim,)), ((), ())), pre...]
    convert_element_type x3 -> x1, other arithmetic: 9.71 us -> 0.9 us  [body(): inputs = (stored.astype(F32) * row_scale[:, None]).astype(BF)]
    unnamed x22 -> x8, local copies, waits for them, and re-layouts: 1.81 us -> 7.82 us
  transfers between devices with their start and end apart: 5 -> 0, of which waited for: 5 -> 0; matrix products, arithmetic and copies ran while one was open for 5% -> 0% of each run, Pallas kernels for 0% -> 0%
where the time goes in v1:
time: 162 us; the launch traced here: 160 us
  Pallas kernels  150 us (93%)
  local copies, waits for them, and re-layouts  8.65 us (5%)
    pallas_call x1, Pallas kernels, body(): pl.pallas_call(kernel, out_shape=(jax.ShapeDtypeStruct((tokens, depth), B...  150 us
    unnamed x8, local copies, waits for them, and re-layouts  7.82 us

profile of v1, /device:TPU:8, one launch (start us, length us, event | category | flops | bytes accessed | tf_op | source)
XLA Modules:
  0.0 160.4 jit_solution(1028986912670606594)
XLA Ops:
  0.6 0.9 multiply_convert_fusion
  1.5 0.8 pad_bitcast_fusion
  2.4 0.7 pad_maximum_fusion.own
  3.0 149.5 %shard_map.93 = (bf16[56,512]{1,0:T(8,128)(2,1)}, bf16[512,1792]{1,0:T(8,128)(2,1)}, bf16[512,1792]{1,0:T(8,128)(2,1)}, bf16[1792,512]{1,0:T(8,128)(2,1)}) custom-call(bf16[2,64,512]{2,1,0:T(8,128)(2,1)} %pad_maximum_fusion.own, bf16[512,1792]{1,0:T(8,128)(2,1)} %wg.1, bf16[512,1792]{1,0:T(8,128)(2,1)} %wu.1, bf16[1792,512]{1,0:T(8,128)(2,1)} %wd.1), custom_call_target="tpu_custom_call" | custom-call | flops 13153337344 | bytes 11010048 | tf_op jit(solution)/shard_map/pallas_call | solution.py:413
  152.6 1.4 copy.14
  154.0 0.0 copy-start.1
  154.0 3.0 %copy.15 = bf16[512,1792]{1,0:T(8,128)(2,1)} copy(bf16[512,1792]{1,0:T(8,128)(2,1)} %get-tuple-element.11) | data formatting | bytes 3670016
  157.0 0.0 copy-done.1
  157.0 0.0 copy-start
  157.0 1.2 copy.16
  158.2 0.9 copy-done
  159.2 1.2 copy.17
Async XLA Ops:
  154.0 3.0 %copy-start.1 = (bf16[512,1792]{1,0:T(8,128)(2,1)S(1)}, bf16[512,1792]{1,0:T(8,128)(2,1)}, u32[]{:S(2)}) copy-start(bf16[512,1792]{1,0:T(8,128)(2,1)} %get-tuple-element.12) | copy-start | bytes 5505028
  157.0 2.2 %copy-start = (bf16[1792,512]{1,0:T(8,128)(2,1)S(1)}, bf16[1792,512]{1,0:T(8,128)(2,1)}, u32[]{:S(2)}) copy-start(bf16[1792,512]{1,0:T(8,128)(2,1)} %get-tuple-element.13) | copy-start | bytes 5505028

commit v2 on v1

v2 whole, which is shorter than its diff:
```python
import jax
import jax.numpy as jnp
from jax import lax
from jax.experimental import pallas as pl
from jax.experimental.pallas import tpu as pltpu
from jax.sharding import PartitionSpec as P

MESH = pl.DeviceIdType.MESH
BF, F32 = jnp.bfloat16, jnp.float32
COPIES = 420
FIRST = "ABABABA"
START = (0, 0, 0, 0, 0, 0, 0)
EARLY = {0: -1, 1: -1, 2: -1}
GU, HG, ALL = slice(0, 256), slice(256, 384), slice(0, 384)


def dot(a, b):
    return lax.dot_general(a, b, (((1,), (0,)), ((), ())), preferred_element_type=F32)


def dot_t(a, b):
    return lax.dot_general(a, b, (((1,), (1,)), ((), ())), preferred_element_type=F32)


def tdot(a, b):
    return lax.dot_general(a, b, (((0,), (0,)), ((), ())), preferred_element_type=F32)


def pack(value):
    half = value.shape[1] // 2
    return jnp.concatenate([value[:, :half], value[:, half:]], axis=0).astype(BF)


def unpack(block):
    value = block.astype(F32)
    rows = value.shape[0] // 2
    return jnp.concatenate([value[:rows], value[rows:]], axis=1)


def kernel(
    stored, scale, out_grad, wg, wu, wd,
    grad_in, grad_gate, grad_up, grad_down,
    blocks, twins, x, px, xt, own_d, peer_gu, peer_d, full_g, full_u,
    part, stage, landed, full, tile_g, tile_u, tile_d, total, tail_s, tail_r, tail_h,
    send_sem, recv_sem, load_sem,
):
    d, t = lax.axis_index("dp"), lax.axis_index("tensor")
    c, y, xl = d % 2, (d // 2) % 4, d // 8
    z, h = t % 8, t // 8
    units = part.shape[0]
    y_up, y_down, y_far = (y + 1) % 4, (y + 3) % 4, (y + 2) % 4
    peer = ((xl * 4 + y) * 2 + 1 - c, t)
    across = (((1 - xl) * 4 + y) * 2 + c, t)
    ups = ((xl * 4 + y_up) * 2 + c, t)
    downs = ((xl * 4 + y_down) * 2 + c, t)
    z_up = (d, h * 8 + (z + 1) % 8)
    z_down = (d, h * 8 + (z + 7) % 8)
    twin = (d, (1 - h) * 8 + z)
    z_up2 = (d, h * 8 + (z + 2) % 8)
    z_down2 = (d, h * 8 + (z + 6) % 8)
    everyone = (z_up2, z_down2, peer, across, ups, downs, z_up, z_down, twin)

    barrier = pltpu.get_barrier_semaphore()
    for device in everyone:
        pl.semaphore_signal(barrier, inc=1, device_id=device, device_id_type=MESH)

    index, sent, loads = {}, [], []

    def send(key, src, dst, device):
        i = index[key] = len(index)
        copy = pltpu.make_async_remote_copy(
            src_ref=src, dst_ref=dst, send_sem=send_sem.at[i], recv_sem=recv_sem.at[i],
            device_id=device, device_id_type=MESH,
        )
        copy.start()
        sent.append(copy)

    def arrive(key, dst):
        i = index[key]
        pltpu.make_async_remote_copy(
            src_ref=dst, dst_ref=dst, send_sem=send_sem.at[i], recv_sem=recv_sem.at[i],
            device_id=peer, device_id_type=MESH,
        ).wait_recv()

    def load(src, dst):
        copy = pltpu.make_async_copy(src, dst, load_sem.at[len(loads)])
        copy.start()
        loads.append(copy)
        return copy

    def cols(u, core):
        return pl.ds(pl.multiple_of(u * 256 + core * 128, 128), 128)

    whole_loads = (load(wg, full_g), load(wu, full_u))
    own_loads = [load(wd.at[cols(u, c), :], own_d.at[u]) for u in range(units)]
    tokens = stored.shape[0]
    same = lax.broadcasted_iota(jnp.int32, (tokens, tokens), 0) == lax.broadcasted_iota(
        jnp.int32, (tokens, tokens), 1
    )
    column = jnp.sum(jnp.where(same, scale[...], 0.0), axis=1, keepdims=True)
    blocks[0, t] = pack((stored[...].astype(F32) * column).astype(BF).astype(F32))
    blocks[1, t] = pack(out_grad[...].astype(F32))

    pl.semaphore_wait(barrier, len(everyone))

    def rank(hh, zz):
        return ((h + hh) % 2) * 8 + zz

    def block_at(a, hh, way, k):
        return blocks.at[a, rank(hh, (z + 8 - k) % 8 if way == "+" else (z + k) % 8)]

    one = {"+": z_up, "-": z_down}
    two = {"+": z_up2, "-": z_down2}
    ways = ("+", "-")
    last_way = ("+", "-")
    by_twin = [[(w, k) for k in (2, 3) for w in ways] + [(last_way[a], 4)] for a in range(2)]

    def to_other_core(a, hh, way, k):
        row = rank(hh, (z + 8 - k) % 8 if way == "+" else (z + k) % 8)
        send(("p", a, hh, way, k), blocks.at[a, row], twins.at[a, row], peer)

    def kick(a):
        block = blocks.at[a, t]
        for way in ways:
            send((1, way, a), block, block, one[way])
        send(("h", a), block, block, twin)
        for way in ways:
            send((2, way, a), block, block, two[way])
        to_other_core(a, 0, "+", 0)

    def gather_near(a):
        for way in ways:
            block = block_at(a, 0, way, 1)
            arrive((1, way, a), block)
            send((3, way, a), block, block, two[way])
            to_other_core(a, 0, way, 1)
        block = block_at(a, 1, "+", 0)
        arrive(("h", a), block)
        for way in ways:
            send(("o", way, a), block, block, one[way])
        to_other_core(a, 1, "+", 0)
        for way in ways:
            block = block_at(a, 0, way, 2)
            arrive((2, way, a), block)
            if way == last_way[a]:
                send((4, way, a), block, block, two[way])
            send(("tw", a, way, 2), block, block, twin)
            to_other_core(a, 0, way, 2)

    def gather_far(a):
        for way in ways:
            arrive(("o", way, a), block_at(a, 1, way, 1))
            to_other_core(a, 1, way, 1)
        for k in (3, 4):
            for way in ways:
                if k == 3 or way == last_way[a]:
                    block = block_at(a, 0, way, k)
                    arrive((k, way, a), block)
                    send(("tw", a, way, k), block, block, twin)
                    to_other_core(a, 0, way, k)

    def gather_last(a):
        for way, k in by_twin[a]:
            arrive(("tw", a, way, k), block_at(a, 1, way, k))
            to_other_core(a, 1, way, k)

    def repack(a):
        def move(src, dst):
            for k in range(8):
                pair = [unpack(src[a, 2 * k + i]) for i in range(2)]
                dst[a, k * 112 : (k + 1) * 112] = jnp.concatenate(pair, axis=0).astype(BF)

        move(blocks, x)
        for hh in range(2):
            for way, k in [("+", 0), ("+", 1), ("-", 1)] + by_twin[a]:
                row = rank(hh, (z + 8 - k) % 8 if way == "+" else (z + k) % 8)
                arrive(("p", a, hh, way, k), twins.at[a, row])
        move(twins, px)

    kick(0)

    def peer_weights(u):
        if u == 0:
            for copy in whole_loads:
                copy.wait()
        send(("wg", u), full_g.at[:, cols(u, 1 - c)], peer_gu.at[u, :, pl.ds(0, 128)], peer)
        send(("wu", u), full_u.at[:, cols(u, 1 - c)], peer_gu.at[u, :, pl.ds(128, 128)], peer)
        send(("wd", u), wd.at[cols(u, 1 - c), :], peer_d.at[u], peer)

    peer_weights(0)

    def transpose():
        for k in range(7):
            xt[:, k * 128 : (k + 1) * 128] = x[0, k * 128 : (k + 1) * 128].T

    gather_near(0)
    kick(1)
    gather_far(0)
    gather_near(1)
    gather_last(0)
    peer_weights(1)
    repack(0)
    gather_far(1)
    peer_weights(2)

    def forward(u, lanes):
        if lanes != HG:
            arrive(("wg", u), peer_gu.at[u, :, pl.ds(0, 128)])
            arrive(("wu", u), peer_gu.at[u, :, pl.ds(128, 128)])
        if lanes != GU:
            own_loads[u].wait()
            arrive(("wd", u), peer_d.at[u])

        def rows_of(i, carry):
            rows = pl.ds(pl.multiple_of(i * 224, 224), 224)
            if lanes != HG:
                own_gu = jnp.concatenate([full_g[:, cols(u, c)], full_u[:, cols(u, c)]], axis=1)
                gu = dot(x[0, rows], own_gu) + dot(px[0, rows], peer_gu[u])
                for j in range(2):
                    part[u, 2 * i + j, :, 0:256] = gu[j * 112 : (j + 1) * 112]
            if lanes != GU:
                hg = dot_t(x[1, rows], own_d[u]) + dot_t(px[1, rows], peer_d[u])
                for j in range(2):
                    part[u, 2 * i + j, :, 256:384] = hg[j * 112 : (j + 1) * 112]
            return carry

        lax.fori_loop(0, 4, rows_of, 0)

    def pointwise(u, summed):
        gate, upper, grad = summed[:, :128], summed[:, 128:256], summed[:, 256:]
        sig = lax.logistic(gate)
        activated = gate * sig
        q = y * 2 + xl
        full[u, c, q, :, 0:128] = (activated * upper).astype(BF)
        full[u, c, q, :, 128:256] = (grad * upper * sig * (1.0 + gate * (1.0 - sig))).astype(BF)
        full[u, c, q, :, 256:384] = (grad * activated).astype(BF)

    def finish(u, lanes, summed):
        if lanes != ALL:
            part[u, 2 * y + xl, :, lanes] = summed
        if lanes != GU:
            pointwise(u, summed if lanes == ALL else part[u, 2 * y + xl])

    def to_peer(u, q, name):
        send(("c", u, name), full.at[u, c, q], full.at[u, c, q], peer)

    def stage_a(u, s, lanes):
        st, rb, to = stage.at[u, :, :, lanes], landed.at[u, :, :, lanes], lanes.start

        def got(k):
            return landed[u, k, :, lanes].astype(F32)

        if s == 0:
            forward(u, lanes)
            for k, q, device in (
                (0, y_far * 2, ups), (1, y_far * 2 + 1, downs),
                (2, y_up * 2 + 1, ups), (3, y_down * 2, downs),
            ):
                stage[u, k, :, lanes] = part[u, q, :, lanes].astype(BF)
                send(("r", u, to, k), st.at[k], rb.at[k], device)
        if s == 1:
            for k, q, device in ((0, y_up * 2, ups), (1, y_down * 2 + 1, downs)):
                arrive(("r", u, to, k), rb.at[k])
                stage[u, 4 + k, :, lanes] = (
                    part[u, q, :, lanes] + landed[u, k, :, lanes].astype(F32)
                ).astype(BF)
                send(("r", u, to, 4 + k), st.at[4 + k], rb.at[4 + k], device)
        if s == 2:
            for k in (2, 3, 4, 5):
                arrive(("r", u, to, k), rb.at[k])
            low = part[u, 2 * y, :, lanes] + (got(4) + got(3))
            high = part[u, 2 * y + 1, :, lanes] + (got(2) + got(5))
            stage[u, 6, :, lanes] = jnp.where(xl == 0, high, low).astype(BF)
            send(("r", u, to, 6), st.at[6], rb.at[6], across)
            part[u, 2 * y + xl, :, lanes] = jnp.where(xl == 0, low, high)
        if s == 3:
            arrive(("r", u, to, 6), rb.at[6])
            finish(u, lanes, part[u, 2 * y + xl, :, lanes] + got(6))
            if lanes == GU:
                return
            mine = full.at[u, c, 2 * y + xl]
            send(("x", u), mine, mine, across)
            send(("u", u, 0), mine, mine, ups)
            send(("d", u, 0), mine, mine, downs)
            to_peer(u, 2 * y + xl, 0)
        if s == 4:
            other = full.at[u, c, 2 * y + 1 - xl]
            arrive(("x", u), other)
            send(("u", u, 1), other, other, ups)
            send(("d", u, 1), other, other, downs)
            to_peer(u, 2 * y + 1 - xl, 1)
        if s == 5:
            for i in range(2):
                e = xl if i == 0 else 1 - xl
                arrive(("u", u, i), full.at[u, c, 2 * y_down + e])
                arrive(("d", u, i), full.at[u, c, 2 * y_up + e])
            low, high = full.at[u, c, 2 * y_down], full.at[u, c, 2 * y_up + 1]
            send(("u", u, 2), low, low, ups)
            send(("d", u, 2), high, high, downs)
            for i in range(2):
                to_peer(u, 2 * y_down + i, 2 + i)
                to_peer(u, 2 * y_up + i, 4 + i)
        if s == 6:
            arrive(("u", u, 2), full.at[u, c, 2 * y_far])
            arrive(("d", u, 2), full.at[u, c, 2 * y_far + 1])
            for i in range(2):
                to_peer(u, 2 * y_far + i, 6 + i)
        if s == 7:
            for i, q in enumerate((
                2 * y + xl, 2 * y + 1 - xl, 2 * y_down, 2 * y_down + 1,
                2 * y_up, 2 * y_up + 1, 2 * y_far, 2 * y_far + 1,
            )):
                arrive(("c", u, i), full.at[u, 1 - c, q])
            backward(u)

    lo, hi = pl.ds(0, 64), pl.ds(64, 48)

    def stage_b(u, s, lanes):
        st, rb, to = stage.at[u, :, :, lanes], landed.at[u, :, :, lanes], lanes.start
        if s == 0:
            forward(u, lanes)
            for k, yy in enumerate((y_far, y_up, y_down, y)):
                stage[u, k, :, lanes] = part[u, yy * 2 + 1 - xl, :, lanes].astype(BF)
                send(("r", u, to, k), st.at[k], rb.at[k], across)
        if s == 1:
            for k, yy in enumerate((y_far, y_up, y_down, y)):
                arrive(("r", u, to, k), rb.at[k])
                summed = part[u, yy * 2 + xl, :, lanes] + landed[u, k, :, lanes].astype(F32)
                if k > 0:
                    part[u, yy * 2 + xl, :, lanes] = summed
                if k < 3:
                    stage[u, 4 + k, :, lanes] = summed.astype(BF)
                if k == 0:
                    send(("f", u, to, 0), st.at[4, lo], rb.at[4, lo], ups)
                    send(("f", u, to, 1), st.at[4, hi], rb.at[4, hi], downs)
                if k == 1:
                    send(("n", u, to, 0), st.at[5, hi], rb.at[5, hi], ups)
                if k == 2:
                    send(("n", u, to, 1), st.at[6, lo], rb.at[6, lo], downs)
        if s == 2:
            arrive(("f", u, to, 0), rb.at[4, lo])
            stage[u, 5, 0:64, lanes] = (
                part[u, y_up * 2 + xl, 0:64, lanes] + landed[u, 4, 0:64, lanes].astype(F32)
            ).astype(BF)
            send(("n", u, to, 2), st.at[5, lo], rb.at[5, lo], ups)
            arrive(("f", u, to, 1), rb.at[4, hi])
            stage[u, 6, 64:112, lanes] = (
                part[u, y_down * 2 + xl, 64:112, lanes] + landed[u, 4, 64:112, lanes].astype(F32)
            ).astype(BF)
            send(("n", u, to, 3), st.at[6, hi], rb.at[6, hi], downs)
        if s == 3:
            arrive(("n", u, to, 0), rb.at[5, hi])
            arrive(("n", u, to, 1), rb.at[6, lo])
            arrive(("n", u, to, 2), rb.at[5, lo])
            arrive(("n", u, to, 3), rb.at[6, hi])
            both = landed[u, 5, :, lanes].astype(F32) + landed[u, 6, :, lanes].astype(F32)
            finish(u, lanes, part[u, 2 * y + xl, :, lanes] + both)
            if lanes == GU:
                return
            mine = full.at[u, c, 2 * y + xl]
            send(("u", u, 0), mine, mine, ups)
            send(("d", u, 0), mine, mine, downs)
            send(("x", u, 0), mine, mine, across)
            to_peer(u, 2 * y + xl, 0)
        if s == 4:
            low, high = full.at[u, c, 2 * y_down + xl], full.at[u, c, 2 * y_up + xl]
            arrive(("u", u, 0), low)
            send(("u", u, 1), low.at[lo], low.at[lo], ups)
            arrive(("d", u, 0), high)
            send(("d", u, 1), high.at[hi], high.at[hi], downs)
            send(("x", u, 1), low, low, across)
            send(("x", u, 2), high, high, across)
            to_peer(u, 2 * y_down + xl, 1)
            to_peer(u, 2 * y_up + xl, 2)
        if s == 5:
            opposite = full.at[u, c, 2 * y_far + xl]
            arrive(("u", u, 1), opposite.at[lo])
            arrive(("d", u, 1), opposite.at[hi])
            send(("x", u, 3), opposite, opposite, across)
            to_peer(u, 2 * y_far + xl, 3)
        order = (y, y_down, y_up, y_far)
        if s == 6:
            for i, yy in enumerate(order):
                arrive(("x", u, i), full.at[u, c, 2 * yy + 1 - xl])
                to_peer(u, 2 * yy + 1 - xl, 4 + i)
        if s == 7:
            for i, yy in enumerate(order):
                arrive(("c", u, i), full.at[u, 1 - c, 2 * yy + xl])
                arrive(("c", u, 4 + i), full.at[u, 1 - c, 2 * yy + 1 - xl])
            backward(u)

    writes = []

    def backward(u):
        wide = slice(u * 256, (u + 1) * 256)

        def lanes(k, groups=pl.ds(0, 8)):
            both = [full[u, core, groups, :, k * 128 : (k + 1) * 128] for core in range(2)]
            return jnp.concatenate([b.reshape(-1, 128) for b in both], axis=1)

        def rows_of(i, carry):
            rows = pl.ds(pl.multiple_of(i * 224, 224), 224)
            groups = pl.ds(2 * i, 2)
            term = dot_t(lanes(1, groups), full_g[:, wide]) + dot_t(lanes(2, groups), full_u[:, wide])
            total[rows] = term if u == 0 else total[rows] + term
            return carry

        lax.fori_loop(0, 4, rows_of, 0)

        def depth_of(i, carry):
            rows = pl.ds(pl.multiple_of(i * 256, 256), 256)
            tile_g[u, rows] = dot(xt[rows], lanes(1)).astype(BF)
            tile_u[u, rows] = dot(xt[rows], lanes(2)).astype(BF)
            return carry

        lax.fori_loop(0, 2, depth_of, 0)
        tile_d[u] = tdot(lanes(0), x[1]).astype(BF)
        writes.append(load(tile_g.at[u], grad_gate.at[:, pl.ds(u * 256, 256)]))
        writes.append(load(tile_u.at[u], grad_up.at[:, pl.ds(u * 256, 256)]))
        writes.append(load(tile_d.at[u], grad_down.at[pl.ds(u * 256, 256), :]))

    def act(u, s, lanes):
        (stage_a if FIRST[u] == "A" else stage_b)(u, s, lanes)

    first_tick = min(EARLY.values(), default=0)
    for tick in range(first_tick, max(START) + 8):
        if tick == 0:
            gather_last(1)
            for u in range(3, units):
                peer_weights(u)
            repack(1)
        works = [(tick - START[u], u, HG if u in EARLY else ALL) for u in range(units)]
        works += [(tick - EARLY[u], u, GU) for u in EARLY if tick - EARLY[u] <= 3]
        for s, u, lanes in sorted(works, key=lambda w: (-w[0], w[1], w[2].start)):
            if 1 <= s <= 6:
                act(u, s, lanes)
        for want in (0, 7):
            for s, u, lanes in works:
                if s == want:
                    act(u, s, lanes)
        if tick == first_tick:
            transpose()

    def block_of(hh, zz):
        return total[pl.ds(pl.multiple_of((hh * 8 + zz) * 56, 8), 56)]

    def tail_send(way, k, hh, add):
        device, zz = (z_up, (z + k) % 8) if way == 0 else (z_down, (z + 8 - k) % 8)
        value = block_of(hh, zz)
        if add:
            arrive(("t", way, k + 1, hh), tail_r.at[way, k, hh])
            value = value + unpack(tail_r[way, k, hh])
        tail_s[way, k - 1, hh] = pack(value)
        send(("t", way, k, hh), tail_s.at[way, k - 1, hh], tail_r.at[way, k - 1, hh], device)

    tail_send(0, 4, 0, False)
    tail_send(1, 4, 1, False)
    tail_send(0, 3, 1, False)
    tail_send(1, 3, 0, False)
    tail_send(0, 3, 0, True)
    tail_send(1, 3, 1, True)
    for k in (2, 1):
        for hh in ((1, 0), (0, 1)):
            for way in range(2):
                tail_send(way, k, hh[way], True)
    for hh in range(2):
        for way in range(2):
            arrive(("t", way, 1, hh), tail_r.at[way, 0, hh])

    def summed(hh):
        return block_of(hh, z) + (unpack(tail_r[0, 0, hh]) + unpack(tail_r[1, 0, hh]))

    tail_h[0] = pack(summed(1 - h))
    send(("twin",), tail_h.at[0], tail_h.at[1], twin)
    mine = summed(h)
    arrive(("twin",), tail_h.at[1])
    grad_in[...] = (mine + unpack(tail_h[1])).astype(BF)

    for copy in sent:
        copy.wait_send()
    for copy in writes:
        copy.wait()


def hand_over(*refs):
    srcs, dsts, held, sem = refs[:4], refs[4:8], refs[8:12], refs[12]
    moves = []
    for i in range(4):
        pieces = 4 if i > 0 else 1
        rows = srcs[i].shape[0] // pieces
        for j in range(pieces):
            at = pl.ds(j * rows, rows)
            moves.append((
                pltpu.make_async_copy(srcs[i].at[at], held[i].at[at], sem.at[0, i, j]),
                pltpu.make_async_copy(held[i].at[at], dsts[i].at[at], sem.at[1, i, j]),
            ))
    for get, _ in moves:
        get.start()
    for get, put in moves:
        get.wait()
        put.start()
    for _, put in moves:
        put.wait()


def body(stored, row_scale, out_grad, gate_weight, up_weight, down_weight):
    tokens, depth = stored.shape
    width = gate_weight.shape[1]
    units = width // 256
    narrow = (112, depth // 2)
    everything = tokens * 16
    anywhere, vmem = pl.BlockSpec(memory_space=pl.ANY), pl.BlockSpec(memory_space=pltpu.VMEM)
    dma = pltpu.SemaphoreType.DMA
    grads = pl.pallas_call(
        kernel,
        out_shape=(
            jax.ShapeDtypeStruct((tokens, depth), BF),
            jax.ShapeDtypeStruct((depth, width), BF),
            jax.ShapeDtypeStruct((depth, width), BF),
            jax.ShapeDtypeStruct((width, depth), BF),
        ),
        in_specs=[vmem, vmem, vmem, anywhere, anywhere, anywhere],
        out_specs=(vmem, anywhere, anywhere, anywhere),
        scratch_shapes=[
            pltpu.VMEM((2, 16, *narrow), BF),
            pltpu.VMEM((2, 16, *narrow), BF),
            pltpu.VMEM((2, everything, depth), BF),
            pltpu.VMEM((2, everything, depth), BF),
            pltpu.VMEM((depth, everything), BF),
            pltpu.VMEM((units, 128, depth), BF),
            pltpu.VMEM((units, depth, 256), BF),
            pltpu.VMEM((units, 128, depth), BF),
            pltpu.VMEM((depth, width), BF),
            pltpu.VMEM((depth, width), BF),
            pltpu.VMEM((units, 8, 112, 384), F32),
            pltpu.VMEM((units, 7, 112, 384), BF),
            pltpu.VMEM((units, 7, 112, 384), BF),
            pltpu.VMEM((units, 2, 8, 112, 384), BF),
            pltpu.VMEM((units, depth, 256), BF),
            pltpu.VMEM((units, depth, 256), BF),
            pltpu.VMEM((units, 256, depth), BF),
            pltpu.VMEM((everything, depth), F32),
            pltpu.VMEM((2, 4, 2, *narrow), BF),
            pltpu.VMEM((2, 4, 2, *narrow), BF),
            pltpu.VMEM((2, *narrow), BF),
            dma((COPIES,)),
            dma((COPIES,)),
            dma((60,)),
        ],
        compiler_params=pltpu.CompilerParams(
            collective_id=0, has_side_effects=True, vmem_limit_bytes=62 * 2**20
        ),
        cost_estimate=pl.CostEstimate(
            flops=16 * everything * depth * width, bytes_accessed=12 * depth * width, transcendentals=0
        ),
    )(stored, row_scale[None, :], out_grad, gate_weight, up_weight, down_weight)
    return pl.pallas_call(
        hand_over,
        out_shape=tuple(jax.ShapeDtypeStruct(g.shape, g.dtype) for g in grads),
        in_specs=[anywhere] * 4,
        out_specs=(anywhere,) * 4,
        scratch_shapes=[pltpu.VMEM(g.shape, g.dtype) for g in grads] + [dma((2, 4, 4))],
        compiler_params=pltpu.CompilerParams(vmem_limit_bytes=62 * 2**20),
    )(*grads)


def solution(mesh):
    placed = (
        P("tensor", "dp"),
        P("tensor"),
        P("tensor", "dp"),
        P("dp", "tensor"),
        P("dp", "tensor"),
        P("tensor", "dp"),
    )
    return jax.shard_map(
        body,
        mesh=mesh,
        in_specs=placed,
        out_specs=(P("tensor", "dp"), P("dp", "tensor"), P("dp", "tensor"), P("tensor", "dp")),
        check_vma=False,
    )
```

time: 162 us -> 151 us (0.932)
  local copies, waits for them, and re-layouts: 8.65 us -> 0 us
    unnamed x8 -> x0, local copies, waits for them, and re-layouts: 7.82 us -> none
    pallas_call x1, Pallas kernels: 150 us -> 144 us  [body(): pl.pallas_call(kernel, out_shape=(jax.ShapeDtypeStruct((tokens, depth), B...]
    pallas_call x0 -> x1, Pallas kernels: none -> 5.13 us  [body(): pl.pallas_call(hand_over, out_shape=tuple((jax.ShapeDtypeStruct(g.shape,...]
where the time goes in v2:
time: 151 us; the launch traced here: 150 us
  Pallas kernels  149 us (99%)
    pallas_call x1, Pallas kernels, body(): pl.pallas_call(kernel, out_shape=(jax.ShapeDtypeStruct((tokens, depth), B...  144 us
    pallas_call x1, Pallas kernels, body(): pl.pallas_call(hand_over, out_shape=tuple((jax.ShapeDtypeStruct(g.shape,...  5.13 us

profile of v2, /device:TPU:8, one launch (start us, length us, event | category | flops | bytes accessed | tf_op | source)
XLA Modules:
  0.0 149.5 jit_solution(13419628274812919473)
XLA Ops:
  0.6 143.8 %shard_map.93 = (bf16[56,512]{1,0:T(8,128)(2,1)}, bf16[512,1792]{1,0:T(8,128)(2,1)}, bf16[512,1792]{1,0:T(8,128)(2,1)}, bf16[1792,512]{1,0:T(8,128)(2,1)}) custom-call(bf16[56,512]{1,0:T(8,128)(2,1)} %stored.1, f32[1,56]{1,0:T(1,128)} %bitcast.1, bf16[56,512]{1,0:T(8,128)(2,1)} %out_grad.1, bf16[512,1792]{1,0:T(8,128)(2,1)} %wg.1, bf16[512,1792]{1,0:T(8,128)(2,1)} %wu.1, ...), custom_call_target="tpu_custom_call" | custom-call | flops 13153337344 | bytes 11010048 | tf_op jit(solution)/shard_map/pallas_call | solution.py:514
  144.4 5.1 %shard_map.94 = (bf16[56,512]{1,0:T(8,128)(2,1)}, bf16[512,1792]{1,0:T(8,128)(2,1)}, bf16[512,1792]{1,0:T(8,128)(2,1)}, bf16[1792,512]{1,0:T(8,128)(2,1)}) custom-call(bf16[56,512]{1,0:T(8,128)(2,1)} %get-tuple-element.8.refs_0_, bf16[512,1792]{1,0:T(8,128)(2,1)} %get-tuple-element.9.refs_1_, bf16[512,1792]{1,0:T(8,128)(2,1)} %get-tuple-element.10.refs_2_, ...), custom_call_target="tpu_custom_call" | custom-call | tf_op jit(solution)/shard_map/pallas_call | solution.py:557

commit v3 on v2

--- a/solution.py
+++ b/solution.py
@@ -10,6 +10,7 @@
 COPIES = 420
 FIRST = "ABABABA"
 START = (0, 0, 0, 0, 0, 0, 0)
+BEHIND = 2
 EARLY = {0: -1, 1: -1, 2: -1}
 GU, HG, ALL = slice(0, 256), slice(256, 384), slice(0, 384)
 
@@ -407,6 +408,11 @@
 
         lax.fori_loop(0, 4, rows_of, 0)
 
+    def weight_grads(u):
+        def lanes(k):
+            both = [full[u, core, :, :, k * 128 : (k + 1) * 128] for core in range(2)]
+            return jnp.concatenate([b.reshape(-1, 128) for b in both], axis=1)
+
         def depth_of(i, carry):
             rows = pl.ds(pl.multiple_of(i * 256, 256), 256)
             tile_g[u, rows] = dot(xt[rows], lanes(1)).astype(BF)
@@ -423,7 +429,7 @@
         (stage_a if FIRST[u] == "A" else stage_b)(u, s, lanes)
 
     first_tick = min(EARLY.values(), default=0)
-    for tick in range(first_tick, max(START) + 8):
+    for tick in range(first_tick, max(START) + 7):
         if tick == 0:
             gather_last(1)
             for u in range(3, units):
@@ -434,12 +440,17 @@
         for s, u, lanes in sorted(works, key=lambda w: (-w[0], w[1], w[2].start)):
             if 1 <= s <= 6:
                 act(u, s, lanes)
-        for want in (0, 7):
-            for s, u, lanes in works:
-                if s == want:
-                    act(u, s, lanes)
-        if tick == first_tick:
+            if s == 6 and u >= BEHIND:
+                act(u - BEHIND, 7, ALL)
+                if u - BEHIND < units - 4:
+                    weight_grads(u - BEHIND)
+        for s, u, lanes in works:
+            if s == 0:
+                act(u, s, lanes)
+        if tick == 0:
             transpose()
+    for u in range(units - BEHIND, units):
+        act(u, 7, ALL)
 
     def block_of(hh, zz):
         return total[pl.ds(pl.multiple_of((hh * 8 + zz) * 56, 8), 56)]
@@ -457,12 +468,15 @@
     tail_send(1, 4, 1, False)
     tail_send(0, 3, 1, False)
     tail_send(1, 3, 0, False)
+    weight_grads(units - 4)
     tail_send(0, 3, 0, True)
     tail_send(1, 3, 1, True)
+    weight_grads(units - 3)
     for k in (2, 1):
         for hh in ((1, 0), (0, 1)):
             for way in range(2):
                 tail_send(way, k, hh[way], True)
+        weight_grads(units - k)
     for hh in range(2):
         for way in range(2):
             arrive(("t", way, 1, hh), tail_r.at[way, 0, hh])

time: 151 us -> 143 us (0.947)
  Pallas kernels: 149 us -> 142 us
    pallas_call x1, Pallas kernels: 144 us -> 137 us  [body(): pl.pallas_call(kernel, out_shape=(jax.ShapeDtypeStruct((tokens, depth), B...]
where the time goes in v3:
time: 143 us
  Pallas kernels  142 us (99%)
    pallas_call x1, Pallas kernels, body(): pl.pallas_call(kernel, out_shape=(jax.ShapeDtypeStruct((tokens, depth), B...  137 us
    pallas_call x1, Pallas kernels, body(): pl.pallas_call(hand_over, out_shape=tuple((jax.ShapeDtypeStruct(g.shape,...  5.13 us

profile of v3, /device:TPU:8, one launch (start us, length us, event | category | flops | bytes accessed | tf_op | source)
XLA Modules:
  0.0 142.8 jit_solution(6433768930903714452)
XLA Ops:
  0.6 137.1 %shard_map.93 = (bf16[56,512]{1,0:T(8,128)(2,1)}, bf16[512,1792]{1,0:T(8,128)(2,1)}, bf16[512,1792]{1,0:T(8,128)(2,1)}, bf16[1792,512]{1,0:T(8,128)(2,1)}) custom-call(bf16[56,512]{1,0:T(8,128)(2,1)} %stored.1, f32[1,56]{1,0:T(1,128)} %bitcast.1, bf16[56,512]{1,0:T(8,128)(2,1)} %out_grad.1, bf16[512,1792]{1,0:T(8,128)(2,1)} %wg.1, bf16[512,1792]{1,0:T(8,128)(2,1)} %wu.1, ...), custom_call_target="tpu_custom_call" | custom-call | flops 13153337344 | bytes 11010048 | tf_op jit(solution)/shard_map/pallas_call | solution.py:528
  137.7 5.1 %shard_map.94 = (bf16[56,512]{1,0:T(8,128)(2,1)}, bf16[512,1792]{1,0:T(8,128)(2,1)}, bf16[512,1792]{1,0:T(8,128)(2,1)}, bf16[1792,512]{1,0:T(8,128)(2,1)}) custom-call(bf16[56,512]{1,0:T(8,128)(2,1)} %get-tuple-element.8.refs_0_, bf16[512,1792]{1,0:T(8,128)(2,1)} %get-tuple-element.9.refs_1_, bf16[512,1792]{1,0:T(8,128)(2,1)} %get-tuple-element.10.refs_2_, ...), custom_call_target="tpu_custom_call" | custom-call | tf_op jit(solution)/shard_map/pallas_call | solution.py:571
